TPU v7x, 256 devices: a whole 4x4x8 slice. The times are simulated.
256 devices in a mesh: sec: 16 (over y, x), bond: 16 (over z, core).
Axes of the slice: x: 4, y: 4, z: 8, core: 2. Of those that a mesh axis runs over, the one named last changes fastest.
Arguments:
- left_vectors: bfloat16 [128, 4096], P(None, 'bond'), may hold values from -6 to 6
- site_tensors: bfloat16 [16, 4096, 4, 4096], P('sec', None, None, 'bond'), may hold values from -0.09375 to 0.09375
- displacement: float32 [128, 216], P('sec'), may hold values from -2.5 to 2.5
- photon_counts: int32 [128, 216], P('sec'), may hold values from 0 to 3
- mode_order: int32 [216], replicated, may hold values from 0 to 215, each once
Outputs:
- log_likelihood: float32 [16, 128], P('sec')
- log_norm: float32 [16, 128], P('sec')
Inputs may be any that keep to these rules, and one draw needn't show every extreme that they name: `mode_order`: each of the 216 modes appears once.
All inputs are finite; a program needn't handle non-finite values.
Results may differ from a plain program's by a relative error of at most 0.0015.
Values may be sent and summed in bfloat16 or wider, within the bound.
A program may use at most 64 MiB of HBM per device.

v0:
```python
import math

import jax
import jax.numpy as jnp
from jax import lax
from jax.sharding import PartitionSpec as P

CUT = 4


epsilon = 1e-06


def joined_along(pieces, dim):
    lengths = list(pieces.shape[1:])
    lengths[dim] *= pieces.shape[0]
    return jnp.moveaxis(pieces, 0, dim).reshape(lengths)


def sent_to_all(x, axis):
    size = lax.axis_size(axis)
    return lax.all_to_all(jnp.broadcast_to(x[None], (size, *x.shape)), axis, 0, 0, tiled=True)


def collect(x, axis, dim):
    return joined_along(sent_to_all(x, axis), dim)


def over_copies(x, axis):
    return sent_to_all(x, axis).sum(axis=0)


def passed_along(x, axis, by):
    size = lax.axis_size(axis)
    pairs = [(i, i + by) for i in range(size) if 0 <= i + by < size]
    return lax.ppermute(x, axis, pairs)


def displacement_table(cutoff):
    table = [
        [[0.0 for degree_slot in range(2 * cutoff - 1)] for col_level in range(cutoff)]
        for row_level in range(cutoff)
    ]
    for row_level in range(cutoff):
        for col_level in range(cutoff):
            lower = min(row_level, col_level)
            upper = max(row_level, col_level)
            excess = upper - lower
            parity = 1.0 if row_level >= col_level else (-1.0) ** excess
            prefactor = math.sqrt(math.factorial(lower) / math.factorial(upper))
            for term in range(lower + 1):
                table[row_level][col_level][excess + 2 * term] += (
                    parity
                    * prefactor
                    * (-1.0) ** term
                    * math.comb(upper, lower - term)
                    / math.factorial(term)
                )
    return table


def displacement_matrix(amplitude):
    table = jnp.asarray(displacement_table(CUT), dtype=jnp.float32)
    power_list = [jnp.ones_like(amplitude)]
    for degree in range(2 * CUT - 2):
        power_list.append(power_list[-1] * amplitude)
    power_stack = jnp.stack(power_list, axis=1)
    poly = jnp.einsum("sp,mnp->smn", power_stack, table, precision=lax.Precision.HIGHEST)
    return jnp.exp(-0.5 * amplitude * amplitude)[:, None, None] * poly


def local(left_vectors, site_tensors, displacement, photon_counts, mode_order):
    full_width = site_tensors.shape[1]
    cutoff = site_tensors.shape[2]
    local_width = site_tensors.shape[3]
    samples = left_vectors.shape[0]
    segment_count = lax.axis_size("sec")
    segment_index = lax.axis_index("sec")
    matrix = site_tensors.reshape(full_width, cutoff * local_width)
    stacked = jnp.stack([displacement, photon_counts.astype(jnp.float32)])
    mode_total = displacement.shape[1]
    window_order = mode_order[:segment_count]
    picker = (window_order[None, :] == jnp.arange(mode_total, dtype=jnp.int32)[:, None]).astype(
        jnp.float32
    )
    ordered = jnp.einsum("rsm,mj->rsj", stacked, picker, precision=lax.Precision.HIGHEST)
    columns = lax.all_to_all(ordered, "sec", split_axis=2, concat_axis=1, tiled=True)
    matrices_all = displacement_matrix(columns[0, :, 0])
    counts_all = columns[1, :, 0]
    levels = jnp.arange(cutoff).astype(jnp.float32)
    blocks = 4
    block_rows = samples // blocks
    incoming_zero = jnp.zeros((block_rows, local_width), jnp.float32)
    extra_zero = jnp.zeros((block_rows,), jnp.float32)

    def add_rows(fragment):
        return jnp.dot(fragment, matrix, preferred_element_type=jnp.float32)

    def one_step(turn_index, state):
        incoming, extra_in, record, norm_record = state
        block_index = turn_index - segment_index
        usable = (block_index >= 0) & (block_index < blocks)
        clamped = jnp.clip(block_index, 0, blocks - 1)
        first_row = clamped * block_rows
        opening = lax.dynamic_slice_in_dim(left_vectors, first_row, block_rows, 0)
        source = jnp.where(segment_index == 0, opening, incoming.astype(jnp.bfloat16))
        factor = jnp.where(segment_index == 0, jnp.ones_like(extra_in), extra_in)
        projected = add_rows(collect(source, "bond", 1))
        projected = (projected * factor[:, None]).reshape(block_rows, cutoff, local_width)
        shifts = lax.dynamic_slice_in_dim(matrices_all, first_row, block_rows, 0)
        counted = lax.dynamic_slice_in_dim(counts_all, first_row, block_rows, 0)
        displaced = jnp.einsum("smn,snb->smb", shifts, projected, precision=lax.Precision.HIGHEST)
        partial_value = jnp.sum(displaced * displaced, axis=2)
        weights = over_copies(partial_value, "bond")
        select = (counted[:, None] == levels[None, :]).astype(jnp.float32)
        chosen_weight = jnp.sum(select * weights, axis=1)
        log_prob = jnp.log(chosen_weight) - jnp.log(jnp.sum(weights, axis=1))
        log_scale = jnp.log(chosen_weight / full_width + epsilon)
        chosen = jnp.sum(select[:, :, None] * displaced, axis=1)
        next_vector = chosen.astype(jnp.bfloat16)
        previous = lax.dynamic_slice_in_dim(record, first_row, block_rows, 0)
        record = lax.dynamic_update_slice_in_dim(
            record, jnp.where(usable, log_prob, previous), first_row, 0
        )
        previous_norm = lax.dynamic_slice_in_dim(norm_record, first_row, block_rows, 0)
        norm_record = lax.dynamic_update_slice_in_dim(
            norm_record, jnp.where(usable, log_scale, previous_norm), first_row, 0
        )
        extra_out = lax.rsqrt(chosen_weight / full_width + epsilon)
        incoming, extra_next = passed_along((next_vector.astype(jnp.float32), extra_out), "sec", 1)
        return (incoming, extra_next, record, norm_record)

    record_zero = jnp.zeros((samples,), jnp.float32)
    final_state = lax.fori_loop(
        0,
        segment_count + blocks - 1,
        one_step,
        (incoming_zero, extra_zero, record_zero, record_zero),
    )
    return (final_state[2][None, :], final_state[3][None, :])


def solution(mesh):
    placed = (P(None, "bond"), P("sec", None, None, "bond"), P("sec", None), P("sec", None), P())
    return jax.shard_map(
        local,
        mesh=mesh,
        in_specs=placed,
        out_specs=(P("sec", None), P("sec", None)),
        check_vma=False,
    )
```

profile of v0, /device:TPU:8, one launch (start us, length us, event | category | flops | bytes accessed | tf_op | source)
XLA Modules:
  0.0 832.0 jit_solution(6361318205880661888)
XLA Ops:
  3.6 7.4 all-to-all-start.2
  11.0 9.4 %copy.26 = bf16[512,8,4,256]{3,1,2,0:T(8,128)(2,1)} copy(bf16[512,8,4,256]{3,2,1,0:T(4,128)(2,1)} %bitcast.49) | data formatting | bytes 16777216
  20.9 810.6 %while.21 = (s32[]{:T(128)}, bf16[32,256]{1,0:T(8,128)(2,1)S(1)}, f32[32]{0:T(128)S(1)}, f32[128]{0:T(128)S(1)}, f32[128]{0:T(128)S(1)}, /*index=5*/s32[]{:T(128...) while((s32[]{:T(128)}, bf16[32,256]{1,0:T(8,128)(2,1)S(1)}, ...), condition=%wide.region_6.7_spmd.clone, body=%wide.region_0.6_spmd.clone.sunk | while | flops 270176768 | bytes 11005419 | solution.py:134
  22.4 8.6 %all-to-all-start = ((bf16[16,32,256]{2,1,0:T(8,128)(2,1)}), bf16[16,32,256]{2,1,0:T(8,128)(2,1)S(1)}, u32[]{:S(2)}, u32[]{:S(2)}) async-start(bf16[16,32,256]{2,1,0:T(8,128)(2,1)} %broadcast_in_dim.75), calls=%async_computation | async-start | bytes 524288 | tf_op jit(solution)/shard_map/while/body/eval_jaxpr/all_to_all | solution.py:22
  31.5 10.7 %all-to-all-done = bf16[16,32,256]{2,1,0:T(8,128)(2,1)S(1)} async-done(((bf16[16,32,256]{2,1,0:T(8,128)(2,1)}), bf16[16,32,256]{2,1,0:T(8,128)(2,1)S(1)}, u32[]{:S(2)}, u32[]{:S(2)}) %all-to-all-start) | async-done | bytes 262176 | tf_op jit(solution)/shard_map/while/body/eval_jaxpr/all_to_all | solution.py:22
  73.9 10.5 %all-to-all-done = bf16[16,32,256]{2,1,0:T(8,128)(2,1)S(1)} async-done(((bf16[16,32,256]{2,1,0:T(8,128)(2,1)}), bf16[16,32,256]{2,1,0:T(8,128)(2,1)S(1)}, u32[]{:S(2)}, u32[]{:S(2)}) %all-to-all-start) | async-done | bytes 262176 | tf_op jit(solution)/shard_map/while/body/eval_jaxpr/all_to_all | solution.py:22
  96.2 5.6 all-to-all-done.1
  116.3 10.5 %all-to-all-done = bf16[16,32,256]{2,1,0:T(8,128)(2,1)S(1)} async-done(((bf16[16,32,256]{2,1,0:T(8,128)(2,1)}), bf16[16,32,256]{2,1,0:T(8,128)(2,1)S(1)}, u32[]{:S(2)}, u32[]{:S(2)}) %all-to-all-start) | async-done | bytes 262176 | tf_op jit(solution)/shard_map/while/body/eval_jaxpr/all_to_all | solution.py:22
  138.6 5.6 all-to-all-done.1
  158.7 10.5 %all-to-all-done = bf16[16,32,256]{2,1,0:T(8,128)(2,1)S(1)} async-done(((bf16[16,32,256]{2,1,0:T(8,128)(2,1)}), bf16[16,32,256]{2,1,0:T(8,128)(2,1)S(1)}, u32[]{:S(2)}, u32[]{:S(2)}) %all-to-all-start) | async-done | bytes 262176 | tf_op jit(solution)/shard_map/while/body/eval_jaxpr/all_to_all | solution.py:22
  181.0 5.6 all-to-all-done.1
  201.1 10.5 %all-to-all-done = bf16[16,32,256]{2,1,0:T(8,128)(2,1)S(1)} async-done(((bf16[16,32,256]{2,1,0:T(8,128)(2,1)}), bf16[16,32,256]{2,1,0:T(8,128)(2,1)S(1)}, u32[]{:S(2)}, u32[]{:S(2)}) %all-to-all-start) | async-done | bytes 262176 | tf_op jit(solution)/shard_map/while/body/eval_jaxpr/all_to_all | solution.py:22
  223.4 5.6 all-to-all-done.1
  243.5 10.5 %all-to-all-done = bf16[16,32,256]{2,1,0:T(8,128)(2,1)S(1)} async-done(((bf16[16,32,256]{2,1,0:T(8,128)(2,1)}), bf16[16,32,256]{2,1,0:T(8,128)(2,1)S(1)}, u32[]{:S(2)}, u32[]{:S(2)}) %all-to-all-start) | async-done | bytes 262176 | tf_op jit(solution)/shard_map/while/body/eval_jaxpr/all_to_all | solution.py:22
  265.8 5.6 all-to-all-done.1
  285.9 10.5 %all-to-all-done = bf16[16,32,256]{2,1,0:T(8,128)(2,1)S(1)} async-done(((bf16[16,32,256]{2,1,0:T(8,128)(2,1)}), bf16[16,32,256]{2,1,0:T(8,128)(2,1)S(1)}, u32[]{:S(2)}, u32[]{:S(2)}) %all-to-all-start) | async-done | bytes 262176 | tf_op jit(solution)/shard_map/while/body/eval_jaxpr/all_to_all | solution.py:22
  308.2 5.6 all-to-all-done.1
  328.3 10.5 %all-to-all-done = bf16[16,32,256]{2,1,0:T(8,128)(2,1)S(1)} async-done(((bf16[16,32,256]{2,1,0:T(8,128)(2,1)}), bf16[16,32,256]{2,1,0:T(8,128)(2,1)S(1)}, u32[]{:S(2)}, u32[]{:S(2)}) %all-to-all-start) | async-done | bytes 262176 | tf_op jit(solution)/shard_map/while/body/eval_jaxpr/all_to_all | solution.py:22
  350.6 5.6 all-to-all-done.1
  370.7 10.5 %all-to-all-done = bf16[16,32,256]{2,1,0:T(8,128)(2,1)S(1)} async-done(((bf16[16,32,256]{2,1,0:T(8,128)(2,1)}), bf16[16,32,256]{2,1,0:T(8,128)(2,1)S(1)}, u32[]{:S(2)}, u32[]{:S(2)}) %all-to-all-start) | async-done | bytes 262176 | tf_op jit(solution)/shard_map/while/body/eval_jaxpr/all_to_all | solution.py:22
  413.1 10.5 %all-to-all-done = bf16[16,32,256]{2,1,0:T(8,128)(2,1)S(1)} async-done(((bf16[16,32,256]{2,1,0:T(8,128)(2,1)}), bf16[16,32,256]{2,1,0:T(8,128)(2,1)S(1)}, u32[]{:S(2)}, u32[]{:S(2)}) %all-to-all-start) | async-done | bytes 262176 | tf_op jit(solution)/shard_map/while/body/eval_jaxpr/all_to_all | solution.py:22
  435.4 5.6 all-to-all-done.1
  455.4 10.5 %all-to-all-done = bf16[16,32,256]{2,1,0:T(8,128)(2,1)S(1)} async-done(((bf16[16,32,256]{2,1,0:T(8,128)(2,1)}), bf16[16,32,256]{2,1,0:T(8,128)(2,1)S(1)}, u32[]{:S(2)}, u32[]{:S(2)}) %all-to-all-start) | async-done | bytes 262176 | tf_op jit(solution)/shard_map/while/body/eval_jaxpr/all_to_all | solution.py:22
  497.8 10.5 %all-to-all-done = bf16[16,32,256]{2,1,0:T(8,128)(2,1)S(1)} async-done(((bf16[16,32,256]{2,1,0:T(8,128)(2,1)}), bf16[16,32,256]{2,1,0:T(8,128)(2,1)S(1)}, u32[]{:S(2)}, u32[]{:S(2)}) %all-to-all-start) | async-done | bytes 262176 | tf_op jit(solution)/shard_map/while/body/eval_jaxpr/all_to_all | solution.py:22
  540.2 10.5 %all-to-all-done = bf16[16,32,256]{2,1,0:T(8,128)(2,1)S(1)} async-done(((bf16[16,32,256]{2,1,0:T(8,128)(2,1)}), bf16[16,32,256]{2,1,0:T(8,128)(2,1)S(1)}, u32[]{:S(2)}, u32[]{:S(2)}) %all-to-all-start) | async-done | bytes 262176 | tf_op jit(solution)/shard_map/while/body/eval_jaxpr/all_to_all | solution.py:22
  582.6 10.5 %all-to-all-done = bf16[16,32,256]{2,1,0:T(8,128)(2,1)S(1)} async-done(((bf16[16,32,256]{2,1,0:T(8,128)(2,1)}), bf16[16,32,256]{2,1,0:T(8,128)(2,1)S(1)}, u32[]{:S(2)}, u32[]{:S(2)}) %all-to-all-start) | async-done | bytes 262176 | tf_op jit(solution)/shard_map/while/body/eval_jaxpr/all_to_all | solution.py:22
  625.0 10.5 %all-to-all-done = bf16[16,32,256]{2,1,0:T(8,128)(2,1)S(1)} async-done(((bf16[16,32,256]{2,1,0:T(8,128)(2,1)}), bf16[16,32,256]{2,1,0:T(8,128)(2,1)S(1)}, u32[]{:S(2)}, u32[]{:S(2)}) %all-to-all-start) | async-done | bytes 262176 | tf_op jit(solution)/shard_map/while/body/eval_jaxpr/all_to_all | solution.py:22
  667.4 10.5 %all-to-all-done = bf16[16,32,256]{2,1,0:T(8,128)(2,1)S(1)} async-done(((bf16[16,32,256]{2,1,0:T(8,128)(2,1)}), bf16[16,32,256]{2,1,0:T(8,128)(2,1)S(1)}, u32[]{:S(2)}, u32[]{:S(2)}) %all-to-all-start) | async-done | bytes 262176 | tf_op jit(solution)/shard_map/while/body/eval_jaxpr/all_to_all | solution.py:22
  709.8 10.5 %all-to-all-done = bf16[16,32,256]{2,1,0:T(8,128)(2,1)S(1)} async-done(((bf16[16,32,256]{2,1,0:T(8,128)(2,1)}), bf16[16,32,256]{2,1,0:T(8,128)(2,1)S(1)}, u32[]{:S(2)}, u32[]{:S(2)}) %all-to-all-start) | async-done | bytes 262176 | tf_op jit(solution)/shard_map/while/body/eval_jaxpr/all_to_all | solution.py:22
  752.2 10.5 %all-to-all-done = bf16[16,32,256]{2,1,0:T(8,128)(2,1)S(1)} async-done(((bf16[16,32,256]{2,1,0:T(8,128)(2,1)}), bf16[16,32,256]{2,1,0:T(8,128)(2,1)S(1)}, u32[]{:S(2)}, u32[]{:S(2)}) %all-to-all-start) | async-done | bytes 262176 | tf_op jit(solution)/shard_map/while/body/eval_jaxpr/all_to_all | solution.py:22
  794.6 10.5 %all-to-all-done = bf16[16,32,256]{2,1,0:T(8,128)(2,1)S(1)} async-done(((bf16[16,32,256]{2,1,0:T(8,128)(2,1)}), bf16[16,32,256]{2,1,0:T(8,128)(2,1)S(1)}, u32[]{:S(2)}, u32[]{:S(2)}) %all-to-all-start) | async-done | bytes 262176 | tf_op jit(solution)/shard_map/while/body/eval_jaxpr/all_to_all | solution.py:22
  816.9 5.6 all-to-all-done.1
  (565 shorter events, 553.1 us)
Async XLA Ops:
  3.6 16.8 %all-to-all-start.2 = ((f32[2,8,16]{1,0,2:T(2,128)}), f32[2,8,16]{1,0,2:T(2,128)S(1)}, u32[]{:S(2)}, u32[]{:S(2)}) async-start(f32[2,8,16]{1,0,2:T(2,128)} %copy.22), calls=%async_computation.2 | async-start | bytes 32768 | tf_op jit(solution)/shard_map/all_to_all | solution.py:87
  22.4 19.8 %all-to-all-start = ((bf16[16,32,256]{2,1,0:T(8,128)(2,1)}), bf16[16,32,256]{2,1,0:T(8,128)(2,1)S(1)}, u32[]{:S(2)}, u32[]{:S(2)}) async-start(bf16[16,32,256]{2,1,0:T(8,128)(2,1)} %broadcast_in_dim.75), calls=%async_computation | async-start | bytes 524288 | tf_op jit(solution)/shard_map/while/body/eval_jaxpr/all_to_all | solution.py:22
  51.9 16.5 %collective-permute-start = (bf16[32,256]{1,0:T(8,128)(2,1)S(1)}, bf16[32,256]{1,0:T(8,128)(2,1)S(1)}, u32[]{:S(2)}, u32[]{:S(2)}) collective-permute-start(bf16[32,256]{1,0:T(8,128)(2,1)S(1)} %get-tuple-element.417), channel_id=1, source_target_pairs={{0,16},{16,32},{32,48},{48,64},{64,80},{80,96},{96,112},{112,128},... | collective-permute-start | bytes 49160 | tf_op jit(solution)/shard_map/while/body/eval_jaxpr/ppermute | solution.py:36
  69.9 14.5 %all-to-all-start = ((bf16[16,32,256]{2,1,0:T(8,128)(2,1)}), bf16[16,32,256]{2,1,0:T(8,128)(2,1)S(1)}, u32[]{:S(2)}, u32[]{:S(2)}) async-start(bf16[16,32,256]{2,1,0:T(8,128)(2,1)} %broadcast_in_dim.75), calls=%async_computation | async-start | bytes 524288 | tf_op jit(solution)/shard_map/while/body/eval_jaxpr/all_to_all | solution.py:22
  94.3 16.5 %collective-permute-start = (bf16[32,256]{1,0:T(8,128)(2,1)S(1)}, bf16[32,256]{1,0:T(8,128)(2,1)S(1)}, u32[]{:S(2)}, u32[]{:S(2)}) collective-permute-start(bf16[32,256]{1,0:T(8,128)(2,1)S(1)} %get-tuple-element.417), channel_id=1, source_target_pairs={{0,16},{16,32},{32,48},{48,64},{64,80},{80,96},{96,112},{112,128},... | collective-permute-start | bytes 49160 | tf_op jit(solution)/shard_map/while/body/eval_jaxpr/ppermute | solution.py:36
  136.7 16.5 %collective-permute-start = (bf16[32,256]{1,0:T(8,128)(2,1)S(1)}, bf16[32,256]{1,0:T(8,128)(2,1)S(1)}, u32[]{:S(2)}, u32[]{:S(2)}) collective-permute-start(bf16[32,256]{1,0:T(8,128)(2,1)S(1)} %get-tuple-element.417), channel_id=1, source_target_pairs={{0,16},{16,32},{32,48},{48,64},{64,80},{80,96},{96,112},{112,128},... | collective-permute-start | bytes 49160 | tf_op jit(solution)/shard_map/while/body/eval_jaxpr/ppermute | solution.py:36
  154.7 14.5 %all-to-all-start = ((bf16[16,32,256]{2,1,0:T(8,128)(2,1)}), bf16[16,32,256]{2,1,0:T(8,128)(2,1)S(1)}, u32[]{:S(2)}, u32[]{:S(2)}) async-start(bf16[16,32,256]{2,1,0:T(8,128)(2,1)} %broadcast_in_dim.75), calls=%async_computation | async-start | bytes 524288 | tf_op jit(solution)/shard_map/while/body/eval_jaxpr/all_to_all | solution.py:22
  179.1 16.5 %collective-permute-start = (bf16[32,256]{1,0:T(8,128)(2,1)S(1)}, bf16[32,256]{1,0:T(8,128)(2,1)S(1)}, u32[]{:S(2)}, u32[]{:S(2)}) collective-permute-start(bf16[32,256]{1,0:T(8,128)(2,1)S(1)} %get-tuple-element.417), channel_id=1, source_target_pairs={{0,16},{16,32},{32,48},{48,64},{64,80},{80,96},{96,112},{112,128},... | collective-permute-start | bytes 49160 | tf_op jit(solution)/shard_map/while/body/eval_jaxpr/ppermute | solution.py:36
  197.1 14.5 %all-to-all-start = ((bf16[16,32,256]{2,1,0:T(8,128)(2,1)}), bf16[16,32,256]{2,1,0:T(8,128)(2,1)S(1)}, u32[]{:S(2)}, u32[]{:S(2)}) async-start(bf16[16,32,256]{2,1,0:T(8,128)(2,1)} %broadcast_in_dim.75), calls=%async_computation | async-start | bytes 524288 | tf_op jit(solution)/shard_map/while/body/eval_jaxpr/all_to_all | solution.py:22
  221.5 16.5 %collective-permute-start = (bf16[32,256]{1,0:T(8,128)(2,1)S(1)}, bf16[32,256]{1,0:T(8,128)(2,1)S(1)}, u32[]{:S(2)}, u32[]{:S(2)}) collective-permute-start(bf16[32,256]{1,0:T(8,128)(2,1)S(1)} %get-tuple-element.417), channel_id=1, source_target_pairs={{0,16},{16,32},{32,48},{48,64},{64,80},{80,96},{96,112},{112,128},... | collective-permute-start | bytes 49160 | tf_op jit(solution)/shard_map/while/body/eval_jaxpr/ppermute | solution.py:36
  239.5 14.5 %all-to-all-start = ((bf16[16,32,256]{2,1,0:T(8,128)(2,1)}), bf16[16,32,256]{2,1,0:T(8,128)(2,1)S(1)}, u32[]{:S(2)}, u32[]{:S(2)}) async-start(bf16[16,32,256]{2,1,0:T(8,128)(2,1)} %broadcast_in_dim.75), calls=%async_computation | async-start | bytes 524288 | tf_op jit(solution)/shard_map/while/body/eval_jaxpr/all_to_all | solution.py:22
  263.9 16.5 %collective-permute-start = (bf16[32,256]{1,0:T(8,128)(2,1)S(1)}, bf16[32,256]{1,0:T(8,128)(2,1)S(1)}, u32[]{:S(2)}, u32[]{:S(2)}) collective-permute-start(bf16[32,256]{1,0:T(8,128)(2,1)S(1)} %get-tuple-element.417), channel_id=1, source_target_pairs={{0,16},{16,32},{32,48},{48,64},{64,80},{80,96},{96,112},{112,128},... | collective-permute-start | bytes 49160 | tf_op jit(solution)/shard_map/while/body/eval_jaxpr/ppermute | solution.py:36
  281.9 14.5 %all-to-all-start = ((bf16[16,32,256]{2,1,0:T(8,128)(2,1)}), bf16[16,32,256]{2,1,0:T(8,128)(2,1)S(1)}, u32[]{:S(2)}, u32[]{:S(2)}) async-start(bf16[16,32,256]{2,1,0:T(8,128)(2,1)} %broadcast_in_dim.75), calls=%async_computation | async-start | bytes 524288 | tf_op jit(solution)/shard_map/while/body/eval_jaxpr/all_to_all | solution.py:22
  306.3 16.5 %collective-permute-start = (bf16[32,256]{1,0:T(8,128)(2,1)S(1)}, bf16[32,256]{1,0:T(8,128)(2,1)S(1)}, u32[]{:S(2)}, u32[]{:S(2)}) collective-permute-start(bf16[32,256]{1,0:T(8,128)(2,1)S(1)} %get-tuple-element.417), channel_id=1, source_target_pairs={{0,16},{16,32},{32,48},{48,64},{64,80},{80,96},{96,112},{112,128},... | collective-permute-start | bytes 49160 | tf_op jit(solution)/shard_map/while/body/eval_jaxpr/ppermute | solution.py:36
  348.7 16.5 %collective-permute-start = (bf16[32,256]{1,0:T(8,128)(2,1)S(1)}, bf16[32,256]{1,0:T(8,128)(2,1)S(1)}, u32[]{:S(2)}, u32[]{:S(2)}) collective-permute-start(bf16[32,256]{1,0:T(8,128)(2,1)S(1)} %get-tuple-element.417), channel_id=1, source_target_pairs={{0,16},{16,32},{32,48},{48,64},{64,80},{80,96},{96,112},{112,128},... | collective-permute-start | bytes 49160 | tf_op jit(solution)/shard_map/while/body/eval_jaxpr/ppermute | solution.py:36
  366.7 14.5 %all-to-all-start = ((bf16[16,32,256]{2,1,0:T(8,128)(2,1)}), bf16[16,32,256]{2,1,0:T(8,128)(2,1)S(1)}, u32[]{:S(2)}, u32[]{:S(2)}) async-start(bf16[16,32,256]{2,1,0:T(8,128)(2,1)} %broadcast_in_dim.75), calls=%async_computation | async-start | bytes 524288 | tf_op jit(solution)/shard_map/while/body/eval_jaxpr/all_to_all | solution.py:22
  391.0 16.5 %collective-permute-start = (bf16[32,256]{1,0:T(8,128)(2,1)S(1)}, bf16[32,256]{1,0:T(8,128)(2,1)S(1)}, u32[]{:S(2)}, u32[]{:S(2)}) collective-permute-start(bf16[32,256]{1,0:T(8,128)(2,1)S(1)} %get-tuple-element.417), channel_id=1, source_target_pairs={{0,16},{16,32},{32,48},{48,64},{64,80},{80,96},{96,112},{112,128},... | collective-permute-start | bytes 49160 | tf_op jit(solution)/shard_map/while/body/eval_jaxpr/ppermute | solution.py:36
  433.4 16.5 %collective-permute-start = (bf16[32,256]{1,0:T(8,128)(2,1)S(1)}, bf16[32,256]{1,0:T(8,128)(2,1)S(1)}, u32[]{:S(2)}, u32[]{:S(2)}) collective-permute-start(bf16[32,256]{1,0:T(8,128)(2,1)S(1)} %get-tuple-element.417), channel_id=1, source_target_pairs={{0,16},{16,32},{32,48},{48,64},{64,80},{80,96},{96,112},{112,128},... | collective-permute-start | bytes 49160 | tf_op jit(solution)/shard_map/while/body/eval_jaxpr/ppermute | solution.py:36
  451.4 14.5 %all-to-all-start = ((bf16[16,32,256]{2,1,0:T(8,128)(2,1)}), bf16[16,32,256]{2,1,0:T(8,128)(2,1)S(1)}, u32[]{:S(2)}, u32[]{:S(2)}) async-start(bf16[16,32,256]{2,1,0:T(8,128)(2,1)} %broadcast_in_dim.75), calls=%async_computation | async-start | bytes 524288 | tf_op jit(solution)/shard_map/while/body/eval_jaxpr/all_to_all | solution.py:22
  475.8 16.5 %collective-permute-start = (bf16[32,256]{1,0:T(8,128)(2,1)S(1)}, bf16[32,256]{1,0:T(8,128)(2,1)S(1)}, u32[]{:S(2)}, u32[]{:S(2)}) collective-permute-start(bf16[32,256]{1,0:T(8,128)(2,1)S(1)} %get-tuple-element.417), channel_id=1, source_target_pairs={{0,16},{16,32},{32,48},{48,64},{64,80},{80,96},{96,112},{112,128},... | collective-permute-start | bytes 49160 | tf_op jit(solution)/shard_map/while/body/eval_jaxpr/ppermute | solution.py:36
  493.8 14.5 %all-to-all-start = ((bf16[16,32,256]{2,1,0:T(8,128)(2,1)}), bf16[16,32,256]{2,1,0:T(8,128)(2,1)S(1)}, u32[]{:S(2)}, u32[]{:S(2)}) async-start(bf16[16,32,256]{2,1,0:T(8,128)(2,1)} %broadcast_in_dim.75), calls=%async_computation | async-start | bytes 524288 | tf_op jit(solution)/shard_map/while/body/eval_jaxpr/all_to_all | solution.py:22
  518.2 16.5 %collective-permute-start = (bf16[32,256]{1,0:T(8,128)(2,1)S(1)}, bf16[32,256]{1,0:T(8,128)(2,1)S(1)}, u32[]{:S(2)}, u32[]{:S(2)}) collective-permute-start(bf16[32,256]{1,0:T(8,128)(2,1)S(1)} %get-tuple-element.417), channel_id=1, source_target_pairs={{0,16},{16,32},{32,48},{48,64},{64,80},{80,96},{96,112},{112,128},... | collective-permute-start | bytes 49160 | tf_op jit(solution)/shard_map/while/body/eval_jaxpr/ppermute | solution.py:36
  536.2 14.5 %all-to-all-start = ((bf16[16,32,256]{2,1,0:T(8,128)(2,1)}), bf16[16,32,256]{2,1,0:T(8,128)(2,1)S(1)}, u32[]{:S(2)}, u32[]{:S(2)}) async-start(bf16[16,32,256]{2,1,0:T(8,128)(2,1)} %broadcast_in_dim.75), calls=%async_computation | async-start | bytes 524288 | tf_op jit(solution)/shard_map/while/body/eval_jaxpr/all_to_all | solution.py:22
  560.6 16.5 %collective-permute-start = (bf16[32,256]{1,0:T(8,128)(2,1)S(1)}, bf16[32,256]{1,0:T(8,128)(2,1)S(1)}, u32[]{:S(2)}, u32[]{:S(2)}) collective-permute-start(bf16[32,256]{1,0:T(8,128)(2,1)S(1)} %get-tuple-element.417), channel_id=1, source_target_pairs={{0,16},{16,32},{32,48},{48,64},{64,80},{80,96},{96,112},{112,128},... | collective-permute-start | bytes 49160 | tf_op jit(solution)/shard_map/while/body/eval_jaxpr/ppermute | solution.py:36
  578.6 14.5 %all-to-all-start = ((bf16[16,32,256]{2,1,0:T(8,128)(2,1)}), bf16[16,32,256]{2,1,0:T(8,128)(2,1)S(1)}, u32[]{:S(2)}, u32[]{:S(2)}) async-start(bf16[16,32,256]{2,1,0:T(8,128)(2,1)} %broadcast_in_dim.75), calls=%async_computation | async-start | bytes 524288 | tf_op jit(solution)/shard_map/while/body/eval_jaxpr/all_to_all | solution.py:22
  603.0 16.5 %collective-permute-start = (bf16[32,256]{1,0:T(8,128)(2,1)S(1)}, bf16[32,256]{1,0:T(8,128)(2,1)S(1)}, u32[]{:S(2)}, u32[]{:S(2)}) collective-permute-start(bf16[32,256]{1,0:T(8,128)(2,1)S(1)} %get-tuple-element.417), channel_id=1, source_target_pairs={{0,16},{16,32},{32,48},{48,64},{64,80},{80,96},{96,112},{112,128},... | collective-permute-start | bytes 49160 | tf_op jit(solution)/shard_map/while/body/eval_jaxpr/ppermute | solution.py:36
  621.0 14.5 %all-to-all-start = ((bf16[16,32,256]{2,1,0:T(8,128)(2,1)}), bf16[16,32,256]{2,1,0:T(8,128)(2,1)S(1)}, u32[]{:S(2)}, u32[]{:S(2)}) async-start(bf16[16,32,256]{2,1,0:T(8,128)(2,1)} %broadcast_in_dim.75), calls=%async_computation | async-start | bytes 524288 | tf_op jit(solution)/shard_map/while/body/eval_jaxpr/all_to_all | solution.py:22
  645.4 16.5 %collective-permute-start = (bf16[32,256]{1,0:T(8,128)(2,1)S(1)}, bf16[32,256]{1,0:T(8,128)(2,1)S(1)}, u32[]{:S(2)}, u32[]{:S(2)}) collective-permute-start(bf16[32,256]{1,0:T(8,128)(2,1)S(1)} %get-tuple-element.417), channel_id=1, source_target_pairs={{0,16},{16,32},{32,48},{48,64},{64,80},{80,96},{96,112},{112,128},... | collective-permute-start | bytes 49160 | tf_op jit(solution)/shard_map/while/body/eval_jaxpr/ppermute | solution.py:36
  687.8 16.5 %collective-permute-start = (bf16[32,256]{1,0:T(8,128)(2,1)S(1)}, bf16[32,256]{1,0:T(8,128)(2,1)S(1)}, u32[]{:S(2)}, u32[]{:S(2)}) collective-permute-start(bf16[32,256]{1,0:T(8,128)(2,1)S(1)} %get-tuple-element.417), channel_id=1, source_target_pairs={{0,16},{16,32},{32,48},{48,64},{64,80},{80,96},{96,112},{112,128},... | collective-permute-start | bytes 49160 | tf_op jit(solution)/shard_map/while/body/eval_jaxpr/ppermute | solution.py:36
  730.2 16.5 %collective-permute-start = (bf16[32,256]{1,0:T(8,128)(2,1)S(1)}, bf16[32,256]{1,0:T(8,128)(2,1)S(1)}, u32[]{:S(2)}, u32[]{:S(2)}) collective-permute-start(bf16[32,256]{1,0:T(8,128)(2,1)S(1)} %get-tuple-element.417), channel_id=1, source_target_pairs={{0,16},{16,32},{32,48},{48,64},{64,80},{80,96},{96,112},{112,128},... | collective-permute-start | bytes 49160 | tf_op jit(solution)/shard_map/while/body/eval_jaxpr/ppermute | solution.py:36
  772.6 16.5 %collective-permute-start = (bf16[32,256]{1,0:T(8,128)(2,1)S(1)}, bf16[32,256]{1,0:T(8,128)(2,1)S(1)}, u32[]{:S(2)}, u32[]{:S(2)}) collective-permute-start(bf16[32,256]{1,0:T(8,128)(2,1)S(1)} %get-tuple-element.417), channel_id=1, source_target_pairs={{0,16},{16,32},{32,48},{48,64},{64,80},{80,96},{96,112},{112,128},... | collective-permute-start | bytes 49160 | tf_op jit(solution)/shard_map/while/body/eval_jaxpr/ppermute | solution.py:36
  814.9 16.5 %collective-permute-start = (bf16[32,256]{1,0:T(8,128)(2,1)S(1)}, bf16[32,256]{1,0:T(8,128)(2,1)S(1)}, u32[]{:S(2)}, u32[]{:S(2)}) collective-permute-start(bf16[32,256]{1,0:T(8,128)(2,1)S(1)} %get-tuple-element.417), channel_id=1, source_target_pairs={{0,16},{16,32},{32,48},{48,64},{64,80},{80,96},{96,112},{112,128},... | collective-permute-start | bytes 49160 | tf_op jit(solution)/shard_map/while/body/eval_jaxpr/ppermute | solution.py:36
  (48 other events, 466.3 us)
where the time goes:
time: 841 us; the launch traced here: 832 us
  waiting for transfers between devices  411 us (49%)
  starting transfers between devices  222 us (26%)
  matrix products  104 us (12%)
  local copies, waits for them, and re-layouts  59.6 us (7%)
  other arithmetic  32.6 us (4%)
    all_to_all x38, waiting for transfers between devices, sent_to_all(): lax.all_to_all(jnp.broadcast_to(x[None], (size, *x.shape)), axis, 0, 0, t...  306 us
    all_to_all x38, starting transfers between devices, sent_to_all(): lax.all_to_all(jnp.broadcast_to(x[None], (size, *x.shape)), axis, 0, 0, t...  139 us
    ppermute x38, waiting for transfers between devices, passed_along(): return lax.ppermute(x, axis, pairs)  105 us
    dot_general x19, matrix products, add_rows(): return jnp.dot(fragment, matrix, preferred_element_type=jnp.float32)  93.7 us
    ppermute x38, starting transfers between devices, passed_along(): return lax.ppermute(x, axis, pairs)  75.8 us
  transfers between devices with their start and end apart: 77, of which 57 were waited for; matrix products, arithmetic and copies ran while one was open for 5% of the time, Pallas kernels for 0%

commit v1 on v0

v1 whole, which is shorter than its diff:
```python
import functools
import math

import jax
import jax.numpy as jnp
from jax import lax
from jax.experimental import pallas as pl
from jax.experimental.pallas import tpu as pltpu
from jax.sharding import PartitionSpec as P

CUT = 4
EPS = 1e-06
ROWS = 16
MESH = pl.DeviceIdType.MESH


def displacement_table(cutoff):
    table = [[[0.0] * (2 * cutoff - 1) for _ in range(cutoff)] for _ in range(cutoff)]
    for row in range(cutoff):
        for col in range(cutoff):
            lower, upper = min(row, col), max(row, col)
            excess = upper - lower
            parity = 1.0 if row >= col else (-1.0) ** excess
            prefactor = math.sqrt(math.factorial(lower) / math.factorial(upper))
            for term in range(lower + 1):
                table[row][col][excess + 2 * term] += (
                    parity * prefactor * (-1.0) ** term * math.comb(upper, lower - term) / math.factorial(term)
                )
    return table


def ring_order(nz):
    return sorted(range(nz), key=lambda d: (min(d, nz - d), d))


def kernel(dims, left, tensor, disp, count, modes, out_ll, out_ln,
           tv, recv, sendv, acc_ref, fac, rows, rrow, prow, ak, aks, gm, gs,
           t_sem, near_sem, far_sem, fnear_sem, ffar_sem, row_sem, ak_sem, p_sem,
           vsend, fsend, rsend, lsend, aksend, psend):
    nsec, nz, blocks, width = dims
    nb = 2 * nz
    chi = nb * width
    order = ring_order(nz)
    far = max(1, (3 * nz) // 8)
    near = nz - far
    s, b = lax.axis_index("sec"), lax.axis_index("bond")
    z, c = b // 2, lax.rem(b, 2)
    sib = 2 * z + 1 - c
    not_first, not_last = s > 0, s < nsec - 1

    def rows_of(q):
        p, other = q % nz, q // nz
        core = c if other == 0 else 1 - c
        return (2 * lax.rem(z + nz - order[p], nz) + core) * width

    loads = []
    for q in range(nb):
        start = pl.multiple_of(rows_of(q), width)
        load = pltpu.make_async_copy(tensor.at[pl.ds(start, width), :], tv.at[q], t_sem.at[q])
        load.start()
        loads.append(load)

    barrier = pltpu.get_barrier_semaphore()

    def greet(sec, bond):
        pl.semaphore_signal(barrier, inc=1, device_id=(sec, bond), device_id_type=MESH)

    def greet_bond(q, carry):
        @pl.when(q != b)
        def _():
            greet(s, q)

        @pl.when(not_last)
        def _():
            greet(s + 1, q)

        @pl.when(not_first)
        def _():
            greet(s - 1, q)

        return carry

    def greet_sec(j, carry):
        @pl.when((j < s - 1) | (j > s + 1))
        def _():
            greet(j, b)

        return carry

    lax.fori_loop(0, nb, greet_bond, 0)
    lax.fori_loop(0, nsec, greet_sec, 0)
    sides = not_first.astype(jnp.int32) + not_last.astype(jnp.int32)

    lane_mode = lax.broadcasted_iota(jnp.int32, disp.shape, 1)

    def pick(j, carry):
        mine = lane_mode == modes[j]
        a = jnp.sum(jnp.where(mine, disp[...], 0.0), axis=1, keepdims=True)
        k = jnp.sum(jnp.where(mine, count[...].astype(jnp.float32), 0.0), axis=1, keepdims=True)
        aks[j, 0] = jnp.broadcast_to(a, (8, 128))
        aks[j, 1] = jnp.broadcast_to(k, (8, 128))
        return carry

    lax.fori_loop(0, nsec, pick, 0)
    ak[s] = aks[s]

    pl.semaphore_wait(barrier, nb - 1 + nb * sides + (nsec - 1 - sides))

    def target(d):
        return 2 * lax.rem(z + d, nz) + c

    def piece_sem(p, t):
        return near_sem.at[t] if p < near else far_sem.at[t]

    def send_pieces(src, t, sec, sem, local):
        for p in reversed(range(nz)):
            if p == 0 and local:
                pltpu.make_async_copy(src, recv.at[t, 0], near_sem.at[t]).start()
                continue
            pltpu.make_async_remote_copy(
                src_ref=src, dst_ref=recv.at[t, p], send_sem=sem, recv_sem=piece_sem(p, t),
                device_id=(sec, target(order[p])), device_id_type=MESH,
            ).start()

    @pl.when(s == 0)
    def _():
        def opening(t, carry):
            send_pieces(left.at[t], t, s, lsend, True)
            return carry

        lax.fori_loop(0, blocks, opening, 0)

    def share(i, carry):
        j = lax.rem(s + 1 + i, nsec)
        pltpu.make_async_remote_copy(
            src_ref=aks.at[j], dst_ref=ak.at[s], send_sem=aksend, recv_sem=ak_sem,
            device_id=(j, b), device_id_type=MESH,
        ).start()
        return carry

    lax.fori_loop(0, nsec - 1, share, 0)

    def wait_bytes(ref, sem):
        pltpu.make_async_copy(ref, ref, sem).wait()

    wait_bytes(ak.at[pl.ds(0, nsec - 1)], ak_sem)

    table = displacement_table(CUT)

    def matrices(t, carry):
        both = ak[pl.ds(2 * t, 2)]
        a = both[:, 0].reshape(ROWS, 128)
        k = both[:, 1].reshape(ROWS, 128)
        power = [None, a]
        for _ in range(2 * CUT - 3):
            power.append(power[-1] * a)
        envelope = jnp.exp(-0.5 * a * a)
        full = [[None] * CUT for _ in range(CUT)]
        for m in range(CUT):
            for n in range(CUT):
                if m < n:
                    continue
                poly = None
                for degree, value in enumerate(table[m][n]):
                    if value != 0.0:
                        term = value if degree == 0 else value * power[degree]
                        poly = term if poly is None else poly + term
                full[m][n] = envelope * poly
                full[n][m] = full[m][n] if (m - n) % 2 == 0 else -full[m][n]
        for m in range(CUT):
            for n in range(CUT):
                gm[t, m * CUT + n] = full[m][n]
        for n in range(CUT):
            g = full[CUT - 1][n]
            for m in reversed(range(CUT - 1)):
                g = jnp.where(k == float(m), full[m][n], g)
            gs[t, n] = g
        return carry

    lax.fori_loop(0, blocks, matrices, 0)

    lane = lax.broadcasted_iota(jnp.int32, (ROWS, 128), 1)
    sample = lax.broadcasted_iota(jnp.int32, (ROWS, 128), 0)

    def dots(acc, t, first, last):
        for q in range(first, last):
            part = jnp.dot(recv[t, q], tv[q], preferred_element_type=jnp.float32)
            acc = part if acc is None else acc + part
        return acc

    def forward(t, first, last, sem):
        pltpu.make_async_remote_copy(
            src_ref=recv.at[t, pl.ds(first, last - first)], dst_ref=recv.at[t, pl.ds(nz + first, last - first)],
            send_sem=fsend, recv_sem=sem.at[t], device_id=(s, sib), device_id_type=MESH,
        ).start()

    def near_part(t):
        wait_bytes(recv.at[t, pl.ds(0, near)], near_sem.at[t])
        forward(t, 0, near, fnear_sem)
        acc = dots(None, t, 0, near)
        wait_bytes(recv.at[t, pl.ds(nz, near)], fnear_sem.at[t])
        acc_ref[...] = dots(acc, t, nz, nz + near)

    fac[...] = jnp.ones_like(fac)
    for load in loads:
        load.wait()
    near_part(0)

    def one_block(t, carry):
        wait_bytes(recv.at[t, pl.ds(near, far)], far_sem.at[t])
        forward(t, near, nz, ffar_sem)
        acc = dots(acc_ref[...], t, near, nz)

        @pl.when(t < blocks - 1)
        def _():
            near_part(t + 1)

        @pl.when(not_first)
        def _():
            wait_bytes(rrow.at[t], row_sem.at[t])
            total = jnp.sum(rrow[t], axis=0)
            weight = jnp.sum(jnp.where(lane == CUT * ROWS + sample, total, 0.0), axis=1, keepdims=True)
            fac[...] = jnp.broadcast_to(lax.rsqrt(weight * (1.0 / chi) + EPS), (ROWS, 128))

        wait_bytes(recv.at[t, pl.ds(nz + near, far)], ffar_sem.at[t])
        acc = dots(acc, t, nz + near, nb) * fac[:, :1]
        proj = [[acc[:, n * width + h * 128:n * width + (h + 1) * 128] for h in range(width // 128)]
                for n in range(CUT)]

        def mix(g):
            return [sum(g[n] * proj[n][h] for n in range(CUT)) for h in range(width // 128)]

        chosen = mix([gs[t, n] for n in range(CUT)])
        sendv[t] = jnp.concatenate(chosen, axis=1).astype(jnp.bfloat16)

        @pl.when(not_last)
        def _():
            send_pieces(sendv.at[t], t, s + 1, vsend, False)

        packed = jnp.zeros((ROWS, 128), jnp.float32)
        k = jnp.concatenate([ak[2 * t, 1], ak[2 * t + 1, 1]], axis=0)
        picked = None
        for m in range(CUT):
            level = mix([gm[t, m * CUT + n] for n in range(CUT)])
            w = jnp.sum(sum(x * x for x in level), axis=1, keepdims=True)
            w = jnp.broadcast_to(w, (ROWS, 128))
            packed = jnp.where(lane == m * ROWS + sample, w, packed)
            picked = w if picked is None else jnp.where(k == float(m), w, picked)
        packed = jnp.where(lane == CUT * ROWS + sample, picked, packed)
        rows[t] = jnp.sum(packed, axis=0, keepdims=True)

        @pl.when(not_last)
        def _():
            for p in reversed(range(nz)):
                for other in range(2):
                    pltpu.make_async_remote_copy(
                        src_ref=rows.at[t], dst_ref=rrow.at[t, other * nz + p], send_sem=rsend, recv_sem=row_sem.at[t],
                        device_id=(s + 1, 2 * lax.rem(z + order[p], nz) + (c if other == 0 else 1 - c)),
                        device_id_type=MESH,
                    ).start()

        return carry

    lax.fori_loop(0, blocks, one_block, 0)

    prow[b] = rows[...]

    def spread(i, carry):
        q = lax.rem(b + 1 + i, nb)
        pltpu.make_async_remote_copy(
            src_ref=rows, dst_ref=prow.at[b], send_sem=psend, recv_sem=p_sem,
            device_id=(s, q), device_id_type=MESH,
        ).start()
        return carry

    lax.fori_loop(0, nb - 1, spread, 0)

    @pl.when(s == 0)
    def _():
        wait_bytes(recv.at[:, pl.ds(1, nz - 1)], lsend)

    @pl.when(not_last)
    def _():
        wait_bytes(recv.at[:, pl.ds(0, nz)], vsend)
        wait_bytes(rrow, rsend)

    wait_bytes(recv.at[:, pl.ds(0, nz)], fsend)
    wait_bytes(aks.at[pl.ds(0, nsec - 1)], aksend)
    wait_bytes(prow.at[pl.ds(0, nb - 1)], p_sem)
    wait_bytes(prow.at[pl.ds(0, nb - 1)], psend)

    samples = blocks * ROWS
    out_lane = lax.broadcasted_iota(jnp.int32, (ROWS, samples), 1)
    out_sample = lax.broadcasted_iota(jnp.int32, (ROWS, samples), 0)
    in_level = (lane < CUT * ROWS) & (lax.rem(lane, ROWS) == sample)

    def finish(t, carry):
        ll, ln = carry
        total = jnp.sum(prow[:, t], axis=0)
        chosen = jnp.sum(jnp.where(lane == CUT * ROWS + sample, total, 0.0), axis=1, keepdims=True)
        every = jnp.sum(jnp.where(in_level, total, 0.0), axis=1, keepdims=True)
        here = out_lane == t * ROWS + out_sample
        ll = jnp.where(here, jnp.log(chosen) - jnp.log(every), ll)
        ln = jnp.where(here, jnp.log(chosen * (1.0 / chi) + EPS), ln)
        return ll, ln

    zero = jnp.zeros((ROWS, samples), jnp.float32)
    ll, ln = lax.fori_loop(0, blocks, finish, (zero, zero))
    out_ll[...] = jnp.sum(ll, axis=0, keepdims=True)
    out_ln[...] = jnp.sum(ln, axis=0, keepdims=True)


def local(left_vectors, site_tensors, displacement, photon_counts, mode_order):
    nsec, nb = lax.axis_size("sec"), lax.axis_size("bond")
    samples, width = left_vectors.shape
    blocks = samples // ROWS
    matrix = site_tensors.reshape(nb * width, CUT * width)
    left = left_vectors.reshape(blocks, ROWS, width)
    vmem = pl.BlockSpec(memory_space=pltpu.VMEM)
    dma = pltpu.SemaphoreType.DMA
    return pl.pallas_call(
        functools.partial(kernel, (nsec, nb // 2, blocks, width)),
        out_shape=[jax.ShapeDtypeStruct((1, samples), jnp.float32)] * 2,
        in_specs=[vmem, pl.BlockSpec(memory_space=pl.ANY), vmem, vmem, pl.BlockSpec(memory_space=pltpu.SMEM)],
        out_specs=[vmem, vmem],
        scratch_shapes=[
            pltpu.VMEM((nb, width, CUT * width), jnp.bfloat16),
            pltpu.VMEM((blocks, nb, ROWS, width), jnp.bfloat16),
            pltpu.VMEM((blocks, ROWS, width), jnp.bfloat16),
            pltpu.VMEM((ROWS, CUT * width), jnp.float32),
            pltpu.VMEM((ROWS, 128), jnp.float32),
            pltpu.VMEM((blocks, 1, 128), jnp.float32),
            pltpu.VMEM((blocks, nb, 1, 128), jnp.float32),
            pltpu.VMEM((nb, blocks, 1, 128), jnp.float32),
            pltpu.VMEM((nsec, 2, 8, 128), jnp.float32),
            pltpu.VMEM((nsec, 2, 8, 128), jnp.float32),
            pltpu.VMEM((blocks, CUT * CUT, ROWS, 128), jnp.float32),
            pltpu.VMEM((blocks, CUT, ROWS, 128), jnp.float32),
            dma((nb,)),
            dma((blocks,)),
            dma((blocks,)),
            dma((blocks,)),
            dma((blocks,)),
            dma((blocks,)),
            dma, dma, dma, dma, dma, dma, dma, dma,
        ],
        compiler_params=pltpu.CompilerParams(
            collective_id=0, has_side_effects=True, vmem_limit_bytes=40 * 2**20
        ),
        cost_estimate=pl.CostEstimate(
            flops=2 * samples * matrix.size, bytes_accessed=2 * matrix.size, transcendentals=samples * 128
        ),
        name="chain",
    )(left, matrix, displacement, photon_counts, mode_order)


def solution(mesh):
    placed = (P(None, "bond"), P("sec", None, None, "bond"), P("sec", None), P("sec", None), P())
    return jax.shard_map(
        local,
        mesh=mesh,
        in_specs=placed,
        out_specs=(P("sec", None), P("sec", None)),
        check_vma=False,
    )
```

time: 841 us -> 196 us (0.23)
  the two profiles are of different devices: /device:TPU:8 before, /device:TPU:31 now
where the time goes in v1:
time: 196 us
  Pallas kernels  181 us (92%)
  local copies, waits for them, and re-layouts  13.8 us (7%)
    pallas_call x1, Pallas kernels, local(): pl.pallas_call(functools.partial(kernel, (nsec, nb // 2, blocks, width)),...  181 us
    unnamed x13, local copies, waits for them, and re-layouts  13.8 us

profile of v1, /device:TPU:31, one launch (start us, length us, event | category | flops | bytes accessed | tf_op | source)
XLA Modules:
  0.0 195.9 jit_solution(16927787558542927239)
XLA Ops:
  0.6 0.0 copy-start.1
  0.6 0.0 copy-start.2
  0.7 0.0 copy-start.3
  0.7 0.0 copy-start.4
  0.7 9.4 %copy.7 = bf16[512,8,4,256]{3,1,2,0:T(8,128)(2,1)} copy(bf16[512,8,4,256]{3,2,1,0:T(4,128)(2,1)} %bitcast.6) | data formatting | bytes 16777216
  10.1 0.0 copy-done.1
  10.1 0.0 copy-done.2
  10.1 0.0 copy-done.3
  10.1 0.0 copy-done.4
  10.1 0.0 copy-start
  10.1 3.4 %copy-done = bf16[512,8,4,256]{3,1,2,0:T(8,128)(2,1)S(1)} copy-done((bf16[512,8,4,256]{3,1,2,0:T(8,128)(2,1)S(1)}, bf16[512,8,4,256]{3,1,2,0:T(8,128)(2,1)}, u32[]{:S(2)}) %copy-start) | copy-done | bytes 8388632
  13.5 181.4 %chain.1 = (f32[1,128]{1,0:T(1,128)S(1)}, f32[1,128]{1,0:T(1,128)S(1)}) custom-call(bf16[8,16,256]{2,1,0:T(8,128)(2,1)S(1)} %bitcast.5, bf16[4096,1024]{1,0:T(8,128)(2,1)S(1)} %bitcast.4, f32[8,216]{1,0:T(8,128)S(1)} %copy-done.2, s32[8,216]{1,0:T(8,128)S(1)} %copy-done.3, s32[216]{0:T(256)S(1)} %copy-done.4), custom_call_target="tpu_custom_call" | custom-call | flops 1073741824 | bytes 8388608 | tf_op jit(solution)/shard_map/chain/pallas_call | solution.py:321
  194.9 0.5 copy.10
  195.4 0.5 copy.11
Async XLA Ops:
  0.6 9.4 %copy-start.1 = (bf16[128,256]{1,0:T(8,128)(2,1)S(1)}, bf16[128,256]{1,0:T(8,128)(2,1)}, u32[]{:S(2)}) copy-start(bf16[128,256]{1,0:T(8,128)(2,1)} %param.5) | copy-start | bytes 196612
  0.6 9.4 %copy-start.2 = (f32[8,216]{1,0:T(8,128)S(1)}, f32[8,216]{1,0:T(8,128)}, u32[]{:S(2)}) copy-start(f32[8,216]{1,0:T(8,128)} %disp.1) | copy-start | bytes 20740
  0.7 9.4 %copy-start.3 = (s32[8,216]{1,0:T(8,128)S(1)}, s32[8,216]{1,0:T(8,128)}, u32[]{:S(2)}) copy-start(s32[8,216]{1,0:T(8,128)} %count.1) | copy-start | bytes 20740
  0.7 9.4 %copy-start.4 = (s32[216]{0:T(256)S(1)}, s32[216]{0:T(256)}, u32[]{:S(2)}) copy-start(s32[216]{0:T(256)} %modes.1) | copy-start | bytes 2596
  10.1 3.4 %copy-start = (bf16[512,8,4,256]{3,1,2,0:T(8,128)(2,1)S(1)}, bf16[512,8,4,256]{3,1,2,0:T(8,128)(2,1)}, u32[]{:S(2)}) copy-start(bf16[512,8,4,256]{3,1,2,0:T(8,128)(2,1)} %copy.7) | copy-start | bytes 25165828

commit v2 on v1

--- a/solution.py
+++ b/solution.py
@@ -34,9 +34,9 @@
 
 
 def kernel(dims, left, tensor, disp, count, modes, out_ll, out_ln,
-           tv, recv, sendv, acc_ref, fac, rows, rrow, prow, ak, aks, gm, gs,
-           t_sem, near_sem, far_sem, fnear_sem, ffar_sem, row_sem, ak_sem, p_sem,
-           vsend, fsend, rsend, lsend, aksend, psend):
+           tv, recv, sendv, acc_ref, nrm, rows, prow, ak, aks, gm, gs,
+           t_sem, near_sem, far_sem, fnear_sem, ak_sem, p_sem,
+           vsend, fsend, lsend, aksend, psend):
     nsec, nz, blocks, width = dims
     nb = 2 * nz
     chi = nb * width
@@ -65,20 +65,24 @@
     def greet(sec, bond):
         pl.semaphore_signal(barrier, inc=1, device_id=(sec, bond), device_id_type=MESH)
 
-    def greet_bond(q, carry):
-        @pl.when(q != b)
-        def _():
-            greet(s, q)
-
-        @pl.when(not_last)
-        def _():
-            greet(s + 1, q)
-
-        @pl.when(not_first)
-        def _():
-            greet(s - 1, q)
-
-        return carry
+    def target(d, other):
+        return 2 * lax.rem(z + d, nz) + (1 - c if other else c)
+
+    fan = [(p, other) for p in reversed(range(nz)) for other in range(2) if p >= near or not other]
+
+    def greet_bond(i, carry):
+        greet(s, lax.rem(b + 1 + i, nb))
+        return carry
+
+    @pl.when(not_last)
+    def _():
+        for p, other in fan:
+            greet(s + 1, target(order[p], other))
+
+    @pl.when(not_first)
+    def _():
+        for p, other in fan:
+            greet(s - 1, target(nz - order[p], other))
 
     def greet_sec(j, carry):
         @pl.when((j < s - 1) | (j > s + 1))
@@ -87,7 +91,7 @@
 
         return carry
 
-    lax.fori_loop(0, nb, greet_bond, 0)
+    lax.fori_loop(0, nb - 1, greet_bond, 0)
     lax.fori_loop(0, nsec, greet_sec, 0)
     sides = not_first.astype(jnp.int32) + not_last.astype(jnp.int32)
 
@@ -104,22 +108,18 @@
     lax.fori_loop(0, nsec, pick, 0)
     ak[s] = aks[s]
 
-    pl.semaphore_wait(barrier, nb - 1 + nb * sides + (nsec - 1 - sides))
-
-    def target(d):
-        return 2 * lax.rem(z + d, nz) + c
-
-    def piece_sem(p, t):
-        return near_sem.at[t] if p < near else far_sem.at[t]
+    pl.semaphore_wait(barrier, nb - 1 + len(fan) * sides + (nsec - 1 - sides))
 
     def send_pieces(src, t, sec, sem, local):
-        for p in reversed(range(nz)):
-            if p == 0 and local:
+        for p, other in fan:
+            slot = other * nz + p
+            if slot == 0 and local:
                 pltpu.make_async_copy(src, recv.at[t, 0], near_sem.at[t]).start()
                 continue
             pltpu.make_async_remote_copy(
-                src_ref=src, dst_ref=recv.at[t, p], send_sem=sem, recv_sem=piece_sem(p, t),
-                device_id=(sec, target(order[p])), device_id_type=MESH,
+                src_ref=src, dst_ref=recv.at[t, slot], send_sem=sem,
+                recv_sem=near_sem.at[t] if p < near else far_sem.at[t],
+                device_id=(sec, target(order[p], other)), device_id_type=MESH,
             ).start()
 
     @pl.when(s == 0)
@@ -182,48 +182,37 @@
     lane = lax.broadcasted_iota(jnp.int32, (ROWS, 128), 1)
     sample = lax.broadcasted_iota(jnp.int32, (ROWS, 128), 0)
 
-    def dots(acc, t, first, last):
+    def dots(acc, squares, t, first, last):
         for q in range(first, last):
-            part = jnp.dot(recv[t, q], tv[q], preferred_element_type=jnp.float32)
+            piece = recv[t, q]
+            part = jnp.dot(piece, tv[q], preferred_element_type=jnp.float32)
             acc = part if acc is None else acc + part
-        return acc
-
-    def forward(t, first, last, sem):
-        pltpu.make_async_remote_copy(
-            src_ref=recv.at[t, pl.ds(first, last - first)], dst_ref=recv.at[t, pl.ds(nz + first, last - first)],
-            send_sem=fsend, recv_sem=sem.at[t], device_id=(s, sib), device_id_type=MESH,
-        ).start()
+            wide = piece.astype(jnp.float32)
+            for h in range(width // 128):
+                half = wide[:, h * 128:(h + 1) * 128]
+                squares = half * half if squares is None else squares + half * half
+        return acc, squares
 
     def near_part(t):
         wait_bytes(recv.at[t, pl.ds(0, near)], near_sem.at[t])
-        forward(t, 0, near, fnear_sem)
-        acc = dots(None, t, 0, near)
+        pltpu.make_async_remote_copy(
+            src_ref=recv.at[t, pl.ds(0, near)], dst_ref=recv.at[t, pl.ds(nz, near)],
+            send_sem=fsend, recv_sem=fnear_sem.at[t], device_id=(s, sib), device_id_type=MESH,
+        ).start()
+        acc, squares = dots(None, None, t, 0, near)
         wait_bytes(recv.at[t, pl.ds(nz, near)], fnear_sem.at[t])
-        acc_ref[...] = dots(acc, t, nz, nz + near)
-
-    fac[...] = jnp.ones_like(fac)
+        acc_ref[...], nrm[...] = dots(acc, squares, t, nz, nz + near)
+
     for load in loads:
         load.wait()
     near_part(0)
 
     def one_block(t, carry):
-        wait_bytes(recv.at[t, pl.ds(near, far)], far_sem.at[t])
-        forward(t, near, nz, ffar_sem)
-        acc = dots(acc_ref[...], t, near, nz)
-
-        @pl.when(t < blocks - 1)
-        def _():
-            near_part(t + 1)
-
-        @pl.when(not_first)
-        def _():
-            wait_bytes(rrow.at[t], row_sem.at[t])
-            total = jnp.sum(rrow[t], axis=0)
-            weight = jnp.sum(jnp.where(lane == CUT * ROWS + sample, total, 0.0), axis=1, keepdims=True)
-            fac[...] = jnp.broadcast_to(lax.rsqrt(weight * (1.0 / chi) + EPS), (ROWS, 128))
-
-        wait_bytes(recv.at[t, pl.ds(nz + near, far)], ffar_sem.at[t])
-        acc = dots(acc, t, nz + near, nb) * fac[:, :1]
+        wait_bytes(recv.at[t, pl.ds(0, 2 * far)], far_sem.at[t])
+        acc, squares = dots(acc_ref[...], nrm[...], t, near, nz)
+        acc, squares = dots(acc, squares, t, nz + near, nb)
+        weight = jnp.sum(squares, axis=1, keepdims=True)
+        acc = acc * jnp.where(not_first, lax.rsqrt(weight * (1.0 / chi) + EPS), 1.0)
         proj = [[acc[:, n * width + h * 128:n * width + (h + 1) * 128] for h in range(width // 128)]
                 for n in range(CUT)]
 
@@ -249,15 +238,9 @@
         packed = jnp.where(lane == CUT * ROWS + sample, picked, packed)
         rows[t] = jnp.sum(packed, axis=0, keepdims=True)
 
-        @pl.when(not_last)
+        @pl.when(t < blocks - 1)
         def _():
-            for p in reversed(range(nz)):
-                for other in range(2):
-                    pltpu.make_async_remote_copy(
-                        src_ref=rows.at[t], dst_ref=rrow.at[t, other * nz + p], send_sem=rsend, recv_sem=row_sem.at[t],
-                        device_id=(s + 1, 2 * lax.rem(z + order[p], nz) + (c if other == 0 else 1 - c)),
-                        device_id_type=MESH,
-                    ).start()
+            near_part(t + 1)
 
         return carry
 
@@ -277,14 +260,13 @@
 
     @pl.when(s == 0)
     def _():
-        wait_bytes(recv.at[:, pl.ds(1, nz - 1)], lsend)
+        wait_bytes(recv.at[:, pl.ds(1, len(fan) - 1)], lsend)
 
     @pl.when(not_last)
     def _():
-        wait_bytes(recv.at[:, pl.ds(0, nz)], vsend)
-        wait_bytes(rrow, rsend)
-
-    wait_bytes(recv.at[:, pl.ds(0, nz)], fsend)
+        wait_bytes(recv.at[:, pl.ds(0, len(fan))], vsend)
+
+    wait_bytes(recv.at[:, pl.ds(0, near)], fsend)
     wait_bytes(aks.at[pl.ds(0, nsec - 1)], aksend)
     wait_bytes(prow.at[pl.ds(0, nb - 1)], p_sem)
     wait_bytes(prow.at[pl.ds(0, nb - 1)], psend)
@@ -330,7 +312,6 @@
             pltpu.VMEM((ROWS, CUT * width), jnp.float32),
             pltpu.VMEM((ROWS, 128), jnp.float32),
             pltpu.VMEM((blocks, 1, 128), jnp.float32),
-            pltpu.VMEM((blocks, nb, 1, 128), jnp.float32),
             pltpu.VMEM((nb, blocks, 1, 128), jnp.float32),
             pltpu.VMEM((nsec, 2, 8, 128), jnp.float32),
             pltpu.VMEM((nsec, 2, 8, 128), jnp.float32),
@@ -340,12 +321,10 @@
             dma((blocks,)),
             dma((blocks,)),
             dma((blocks,)),
-            dma((blocks,)),
-            dma((blocks,)),
-            dma, dma, dma, dma, dma, dma, dma, dma,
+            dma, dma, dma, dma, dma, dma, dma,
         ],
         compiler_params=pltpu.CompilerParams(
-            collective_id=0, has_side_effects=True, vmem_limit_bytes=40 * 2**20
+            collective_id=0, has_side_effects=True, vmem_limit_bytes=60 * 2**20
         ),
         cost_estimate=pl.CostEstimate(
             flops=2 * samples * matrix.size, bytes_accessed=2 * matrix.size, transcendentals=samples * 128

time: 196 us -> 182 us (0.929)
  Pallas kernels: 181 us -> 169 us
  local copies, waits for them, and re-layouts: 13.8 us -> 11.6 us
    pallas_call x1, Pallas kernels: 181 us -> 169 us  [local(): pl.pallas_call(functools.partial(kernel, (nsec, nb // 2, blocks, width)),...]
    unnamed x13 -> x3, local copies, waits for them, and re-layouts: 13.8 us -> 11.6 us
where the time goes in v2:
time: 182 us; the launch traced here: 181 us
  Pallas kernels  169 us (93%)
  local copies, waits for them, and re-layouts  11.6 us (6%)
    pallas_call x1, Pallas kernels, local(): pl.pallas_call(functools.partial(kernel, (nsec, nb // 2, blocks, width)),...  169 us
    unnamed x3, local copies, waits for them, and re-layouts  11.6 us

profile of v2, /device:TPU:31, one launch (start us, length us, event | category | flops | bytes accessed | tf_op | source)
XLA Modules:
  0.0 181.5 jit_solution(17506745963689851688)
XLA Ops:
  0.6 9.4 %copy.7 = bf16[512,8,4,256]{3,1,2,0:T(8,128)(2,1)} copy(bf16[512,8,4,256]{3,2,1,0:T(4,128)(2,1)} %bitcast.5) | data formatting | bytes 16777216
  10.0 169.2 %chain.1 = (f32[1,128]{1,0:T(1,128)}, f32[1,128]{1,0:T(1,128)}) custom-call(bf16[8,16,256]{2,1,0:T(8,128)(2,1)} %bitcast.6, bf16[4096,1024]{1,0:T(8,128)(2,1)} %bitcast.4, f32[8,216]{1,0:T(8,128)} %disp.1, s32[8,216]{1,0:T(8,128)} %count.1, s32[216]{0:T(256)} %modes.1), custom_call_target="tpu_custom_call" | custom-call | flops 1073741824 | bytes 8388608 | tf_op jit(solution)/shard_map/chain/pallas_call | solution.py:303
  179.2 1.1 copy.10
  180.4 1.1 copy.11
